TPU v7x, 512 devices: a whole 4x8x8 slice. The times are simulated.
512 devices in a mesh: dp: 16 (over z, core), seq: 32 (over x, y).
Axes of the slice: x: 4, y: 8, z: 8, core: 2. Of those that a mesh axis runs over, the one named last changes fastest.
Arguments:
- queries: bfloat16 [65536, 4096], P(('dp', 'seq')), may hold values from -6 to 6
- keys: bfloat16 [65536, 512], P(('dp', 'seq')), may hold values from -6 to 6
- values: bfloat16 [65536, 512], P(('dp', 'seq')), may hold values from -6 to 6
- d_out: bfloat16 [65536, 4096], P(('dp', 'seq')), may hold values from -6 to 6
- doc_lengths: int32 [171], replicated, may hold values from 1 to 768, as said below
Outputs:
- d_queries: bfloat16 [65536, 4096], P(('dp', 'seq'))
- key_gradient: bfloat16 [65536, 512], P(('dp', 'seq'))
- value_gradient: bfloat16 [65536, 512], P(('dp', 'seq'))
Inputs may be any that keep to these rules, and one draw needn't show every extreme that they name: `doc_lengths`: lengths of the 171 documents in order; they sum to 65536, and the longest has exactly 768 tokens.
All inputs are finite; a program needn't handle non-finite values.
Results may differ from a plain program's by a relative error of at most 0.008.
Values may be sent and summed in bfloat16 or wider, within the bound.
A program may use at most 64 MiB of HBM per device.

v0:
```python
import math
import jax
import jax.numpy as jnp
from jax import lax
from jax.sharding import PartitionSpec as P

HEAD_SIZE = 128
GROUP = 8
DOC_MOST = 768


def from_behind(value, axis, steps):
    count = lax.axis_size(axis)
    leading, last = (max(0, -steps), min(count, count - steps))
    return lax.ppermute(value, axis, [(source, source + steps) for source in range(leading, last)])


def as_sent(shard):
    return jax.tree.map(lambda a: a.astype(jnp.bfloat16) if a.dtype == jnp.float32 else a, shard)


def doc_index(positions, doc_ends):
    return jnp.sum((positions[:, None] >= doc_ends[None, :]).astype(jnp.int32), axis=1)


def block_grads(q_rows, key_rows, value_rows, grad_rows, allowed, score_scale):
    scores = jnp.dot(q_rows, key_rows.T, preferred_element_type=jnp.float32) * score_scale
    scores = jnp.where(allowed, scores, -1e30)
    row_max = jnp.max(scores, axis=1, keepdims=True)
    exp_scores = jnp.exp(scores - row_max)
    attn_probs = exp_scores / jnp.sum(exp_scores, axis=1, keepdims=True)
    probs_low = attn_probs.astype(jnp.bfloat16)
    grad_probs = jnp.dot(grad_rows, value_rows.T, preferred_element_type=jnp.float32)
    row_delta = jnp.sum(attn_probs * grad_probs, axis=1, keepdims=True)
    grad_scores = (attn_probs * (grad_probs - row_delta) * score_scale).astype(jnp.bfloat16)
    grad_q = jnp.dot(grad_scores, key_rows, preferred_element_type=jnp.float32)
    grad_k = jnp.dot(grad_scores.T, q_rows, preferred_element_type=jnp.float32)
    grad_v = jnp.dot(probs_low.T, grad_rows, preferred_element_type=jnp.float32)
    return (grad_q, grad_k, grad_v)


def local(queries, keys, values, d_out, doc_lengths):
    tok_rows, q_width = queries.shape
    seq_devices = lax.axis_size("seq")
    kv_width = keys.shape[1]
    kv_heads = kv_width // HEAD_SIZE
    doc_ends = jnp.cumsum(doc_lengths)
    score_scale = 1.0 / math.sqrt(HEAD_SIZE)
    block_rows = tok_rows * seq_devices
    spread_k = jnp.broadcast_to(
        keys.reshape(tok_rows, kv_heads, 1, HEAD_SIZE), (tok_rows, kv_heads, GROUP, HEAD_SIZE)
    ).reshape(tok_rows, q_width)
    spread_v = jnp.broadcast_to(
        values.reshape(tok_rows, kv_heads, 1, HEAD_SIZE), (tok_rows, kv_heads, GROUP, HEAD_SIZE)
    ).reshape(tok_rows, q_width)
    head_q, head_g, head_k, head_v = (
        lax.all_to_all(queries, "seq", split_axis=1, concat_axis=0, tiled=True),
        lax.all_to_all(d_out, "seq", split_axis=1, concat_axis=0, tiled=True),
        lax.all_to_all(spread_k, "seq", split_axis=1, concat_axis=0, tiled=True),
        lax.all_to_all(spread_v, "seq", split_axis=1, concat_axis=0, tiled=True),
    )
    tail_pair = jnp.stack([head_k, head_v])
    prior_pair = from_behind(tail_pair, "dp", 1)
    all_k = jnp.concatenate([prior_pair[0], head_k], axis=0)
    all_v = jnp.concatenate([prior_pair[1], head_v], axis=0)
    block_start = lax.axis_index("dp") * block_rows
    query_span = min(512, block_rows)
    key_window = query_span + DOC_MOST
    steps_count = block_rows // query_span
    query_pos = block_start + jnp.arange(block_rows, dtype=jnp.int32)
    key_pos = block_start - block_rows + jnp.arange(block_rows + block_rows, dtype=jnp.int32)
    query_docs = doc_index(query_pos, doc_ends)
    key_docs = doc_index(key_pos, doc_ends)

    def step(totals, step_index):
        acc_k, acc_v = totals
        row_start = step_index * query_span
        key_start = row_start + block_rows - DOC_MOST
        q_rows = lax.dynamic_slice_in_dim(head_q, row_start, query_span, 0)
        g_rows = lax.dynamic_slice_in_dim(head_g, row_start, query_span, 0)
        key_rows = lax.dynamic_slice_in_dim(all_k, key_start, key_window, 0)
        value_rows = lax.dynamic_slice_in_dim(all_v, key_start, key_window, 0)
        q_pos = lax.dynamic_slice_in_dim(query_pos, row_start, query_span, 0)
        k_pos = lax.dynamic_slice_in_dim(key_pos, key_start, key_window, 0)
        q_docs = lax.dynamic_slice_in_dim(query_docs, row_start, query_span, 0)
        k_docs = lax.dynamic_slice_in_dim(key_docs, key_start, key_window, 0)
        allowed = (
            (q_docs[:, None] == k_docs[None, :])
            & (k_pos[None, :] <= q_pos[:, None])
            & (k_pos[None, :] >= 0)
        )
        grad_q, grad_k, grad_v = block_grads(
            q_rows, key_rows, value_rows, g_rows, allowed, score_scale
        )
        acc_k = lax.dynamic_update_slice_in_dim(
            acc_k, lax.dynamic_slice_in_dim(acc_k, key_start, key_window, 0) + grad_k, key_start, 0
        )
        acc_v = lax.dynamic_update_slice_in_dim(
            acc_v, lax.dynamic_slice_in_dim(acc_v, key_start, key_window, 0) + grad_v, key_start, 0
        )
        return ((acc_k, acc_v), grad_q.astype(jnp.bfloat16))

    empty_acc = jnp.zeros((block_rows + block_rows, HEAD_SIZE), jnp.float32)
    (acc_k, acc_v), q_blocks = lax.scan(
        step, (empty_acc, empty_acc), jnp.arange(steps_count, dtype=jnp.int32)
    )
    grads_q = q_blocks.reshape(block_rows, HEAD_SIZE)
    back_pair = from_behind(
        jnp.stack([acc_k[:block_rows], acc_v[:block_rows]]).astype(jnp.bfloat16), "dp", -1
    ).astype(jnp.float32)
    own_k = acc_k[block_rows:]
    own_v = acc_v[block_rows:]
    split_at = block_rows - block_rows
    term_k = jnp.concatenate([own_k[:split_at], own_k + back_pair[0]], axis=0)
    term_v = jnp.concatenate([own_v[:split_at], own_v + back_pair[1]], axis=0)
    tok_dq = lax.all_to_all(grads_q, "seq", split_axis=0, concat_axis=1, tiled=True)
    tok_k, tok_v = (
        lax.all_to_all(as_sent(term_k), "seq", split_axis=0, concat_axis=1, tiled=True).astype(
            term_k.dtype
        ),
        lax.all_to_all(as_sent(term_v), "seq", split_axis=0, concat_axis=1, tiled=True).astype(
            term_v.dtype
        ),
    )
    key_gradient = (
        jnp.sum(tok_k.reshape(tok_rows, kv_heads, GROUP, HEAD_SIZE), axis=2)
        .reshape(tok_rows, kv_width)
        .astype(jnp.bfloat16)
    )
    value_gradient = (
        jnp.sum(tok_v.reshape(tok_rows, kv_heads, GROUP, HEAD_SIZE), axis=2)
        .reshape(tok_rows, kv_width)
        .astype(jnp.bfloat16)
    )
    return (tok_dq, key_gradient, value_gradient)


def solution(mesh):
    in_specs = (
        P(("dp", "seq"), None),
        P(("dp", "seq"), None),
        P(("dp", "seq"), None),
        P(("dp", "seq"), None),
        P(),
    )
    out_specs = (P(("dp", "seq"), None), P(("dp", "seq"), None), P(("dp", "seq"), None))
    return jax.shard_map(local, mesh=mesh, in_specs=in_specs, out_specs=out_specs, check_vma=False)
```

profile of v0, /device:TPU:448, one launch (start us, length us, event | category | flops | bytes accessed | tf_op | source)
XLA Modules:
  0.0 370.4 jit_solution(15627165320955770170)
XLA Ops:
  2.9 10.0 %all-to-all-start.2 = ((bf16[128,32,128]{2,0,1:T(8,128)(2,1)}), bf16[128,32,128]{2,0,1:T(8,128)(2,1)S(1)}, u32[]{:S(2)}, u32[]{:S(2)}) async-start(bf16[128,32,128]{2,0,1:T(8,128)(2,1)} %bitcast.9), calls=%async_computation.2 | async-start | bytes 2097152 | tf_op jit(solution)/shard_map/all_to_all | solution.py:60
  12.9 28.6 %all-to-all-done.2 = bf16[128,32,128]{2,0,1:T(8,128)(2,1)S(1)} async-done(((bf16[128,32,128]{2,0,1:T(8,128)(2,1)}), bf16[128,32,128]{2,0,1:T(8,128)(2,1)S(1)}, u32[]{:S(2)}, u32[]{:S(2)}) %all-to-all-start.2) | async-done | bytes 1048608 | tf_op jit(solution)/shard_map/all_to_all | solution.py:60
  42.7 5.1 %all-to-all-start.1 = ((bf16[128,32,128]{2,0,1:T(8,128)(2,1)}), bf16[128,32,128]{2,0,1:T(8,128)(2,1)S(1)}, u32[]{:S(2)}, u32[]{:S(2)}) async-start(bf16[128,32,128]{2,0,1:T(8,128)(2,1)} %bitcast.99), calls=%async_computation.1 | async-start | bytes 2097152 | tf_op jit(solution)/shard_map/all_to_all | solution.py:59
  49.1 27.0 %all-to-all-done.1 = bf16[128,32,128]{2,0,1:T(8,128)(2,1)S(1)} async-done(((bf16[128,32,128]{2,0,1:T(8,128)(2,1)}), bf16[128,32,128]{2,0,1:T(8,128)(2,1)S(1)}, u32[]{:S(2)}, u32[]{:S(2)}) %all-to-all-start.1) | async-done | bytes 1048608 | tf_op jit(solution)/shard_map/all_to_all | solution.py:59
  76.1 5.0 %all-to-all-start = ((bf16[128,32,128]{2,0,1:T(8,128)(2,1)}), bf16[128,32,128]{2,0,1:T(8,128)(2,1)}, u32[]{:S(2)}, u32[]{:S(2)}) async-start(bf16[128,32,128]{2,0,1:T(8,128)(2,1)} %copy_bitcast_fusion.1), calls=%async_computation | async-start | bytes 2097152 | tf_op jit(solution)/shard_map/all_to_all | solution.py:57
  86.0 2.5 copy_bitcast_fusion
  88.5 21.0 %all-to-all-done = bf16[128,32,128]{2,0,1:T(8,128)(2,1)} async-done(((bf16[128,32,128]{2,0,1:T(8,128)(2,1)}), bf16[128,32,128]{2,0,1:T(8,128)(2,1)}, u32[]{:S(2)}, u32[]{:S(2)}) %all-to-all-start) | async-done | bytes 1048608 | tf_op jit(solution)/shard_map/all_to_all | solution.py:57
  109.4 5.0 %all-to-all-start.3 = ((bf16[128,32,128]{2,0,1:T(8,128)(2,1)}), bf16[128,32,128]{2,0,1:T(8,128)(2,1)}, u32[]{:S(2)}, u32[]{:S(2)}) async-start(bf16[128,32,128]{2,0,1:T(8,128)(2,1)} %copy_bitcast_fusion), calls=%async_computation.3 | async-start | bytes 2097152 | tf_op jit(solution)/shard_map/all_to_all | solution.py:58
  116.6 2.2 pad_maximum_fusion.1
  118.8 23.9 %all-to-all-done.3 = bf16[128,32,128]{2,0,1:T(8,128)(2,1)} async-done(((bf16[128,32,128]{2,0,1:T(8,128)(2,1)}), bf16[128,32,128]{2,0,1:T(8,128)(2,1)}, u32[]{:S(2)}, u32[]{:S(2)}) %all-to-all-start.3) | async-done | bytes 1048608 | tf_op jit(solution)/shard_map/all_to_all | solution.py:58
  142.8 2.2 broadcast_in_dim.52.clone
  145.0 2.2 broadcast_in_dim.52
  147.2 113.3 %while.18 = (s32[]{:T(128)}, f32[8192,128]{1,0:T(8,128)}, f32[8192,128]{1,0:T(8,128)}, bf16[8,512,128]{2,1,0:T(8,128)(2,1)}, s32[8]{0:T(128)S(1)}, /*index=5*/s3...) while((s32[]{:T(128)}, f32[8192,128]{1,0:T(8,128)}, ...), condition=%wide.region_8.9_spmd, body=%wide.region_4.0_spmd.sunk | while | flops 853671680 | bytes 26610516 | solution.py:104
  153.9 2.1 fusion.56
  156.0 2.8 fusion.55
  158.8 2.6 fusion.54
  162.9 2.0 fusion.52
  168.0 2.1 fusion.56
  170.2 2.8 fusion.55
  173.0 2.5 fusion.54
  182.2 2.1 fusion.56
  184.4 2.8 fusion.55
  187.1 2.6 fusion.54
  196.4 2.1 fusion.56
  198.5 2.8 fusion.55
  201.3 2.6 fusion.54
  210.6 2.1 fusion.56
  212.7 2.8 fusion.55
  215.5 2.6 fusion.54
  219.6 2.0 fusion.52
  224.7 2.1 fusion.56
  226.9 2.8 fusion.55
  229.7 2.5 fusion.54
  233.8 2.0 fusion.52
  238.9 2.1 fusion.56
  241.0 2.8 fusion.55
  243.8 2.5 fusion.54
  253.0 2.1 fusion.56
  255.2 2.8 fusion.55
  258.0 2.6 fusion.54
  267.4 4.9 %all-to-all-start.4 = ((bf16[32,128,128]{2,1,0:T(8,128)(2,1)}), bf16[32,128,128]{2,1,0:T(8,128)(2,1)S(1)}, u32[]{:S(2)}, u32[]{:S(2)}) async-start(bf16[32,128,128]{2,1,0:T(8,128)(2,1)} %bitcast.18), calls=%async_computation.4 | async-start | bytes 2097152 | tf_op jit(solution)/shard_map/all_to_all | solution.py:116
  272.3 18.9 %collective-permute-done.1 = bf16[2,4096,128]{2,1,0:T(8,128)(2,1)} collective-permute-done((bf16[2,4096,128]{2,1,0:T(8,128)(2,1)}, bf16[2,4096,128]{2,1,0:T(8,128)(2,1)}, u32[]{:S(2)}, u32[]{:S(2)}) %collective-permute-start.1) | collective-permute-done | bytes 2097184 | tf_op jit(solution)/shard_map/ppermute | solution.py:15
  293.1 3.2 fusion.23
  296.3 3.9 %all-to-all-done.4 = bf16[32,128,128]{2,1,0:T(8,128)(2,1)S(1)} async-done(((bf16[32,128,128]{2,1,0:T(8,128)(2,1)}), bf16[32,128,128]{2,1,0:T(8,128)(2,1)S(1)}, u32[]{:S(2)}, u32[]{:S(2)}) %all-to-all-start.4) | async-done | bytes 1048608 | tf_op jit(solution)/shard_map/all_to_all | solution.py:116
  300.2 35.8 %all_to_all.121 = bf16[32,128,128]{2,1,0:T(8,128)(2,1)} all-to-all(bf16[32,128,128]{2,1,0:T(8,128)(2,1)S(1)} %bitcast.98), channel_id=1, replica_groups=mesh['dp'=16,'seq'=32] {'seq'}, dimensions={0} | all-to-all | bytes 2097152 | tf_op jit(solution)/shard_map/all_to_all | solution.py:118
  336.0 5.1 %all-to-all-start.6 = ((bf16[32,128,128]{2,1,0:T(8,128)(2,1)}), bf16[32,128,128]{2,1,0:T(8,128)(2,1)S(1)}, u32[]{:S(2)}, u32[]{:S(2)}) async-start(bf16[32,128,128]{2,1,0:T(8,128)(2,1)} %bitcast.29), calls=%async_computation.6 | async-start | bytes 2097152 | tf_op jit(solution)/shard_map/all_to_all | solution.py:121
  342.5 2.4 copy.39
  345.9 23.5 %all-to-all-done.6 = bf16[32,128,128]{2,1,0:T(8,128)(2,1)S(1)} async-done(((bf16[32,128,128]{2,1,0:T(8,128)(2,1)}), bf16[32,128,128]{2,1,0:T(8,128)(2,1)S(1)}, u32[]{:S(2)}, u32[]{:S(2)}) %all-to-all-start.6) | async-done | bytes 1048608 | tf_op jit(solution)/shard_map/all_to_all | solution.py:121
  (112 shorter events, 65.7 us)
Async XLA Ops:
  0.6 47.2 %copy-start = (bf16[128,4096]{1,0:T(8,128)(2,1)S(1)}, bf16[128,4096]{1,0:T(8,128)(2,1)}, u32[]{:S(2)}) copy-start(bf16[128,4096]{1,0:T(8,128)(2,1)} %param.7) | copy-start | bytes 3145732
  0.6 12.2 %copy-start.3 = (bf16[128,512]{1,0:T(8,128)(2,1)S(1)}, bf16[128,512]{1,0:T(8,128)(2,1)}, u32[]{:S(2)}) copy-start(bf16[128,512]{1,0:T(8,128)(2,1)} %param.8) | copy-start | bytes 393220
  2.9 38.6 %all-to-all-start.2 = ((bf16[128,32,128]{2,0,1:T(8,128)(2,1)}), bf16[128,32,128]{2,0,1:T(8,128)(2,1)S(1)}, u32[]{:S(2)}, u32[]{:S(2)}) async-start(bf16[128,32,128]{2,0,1:T(8,128)(2,1)} %bitcast.9), calls=%async_computation.2 | async-start | bytes 2097152 | tf_op jit(solution)/shard_map/all_to_all | solution.py:60
  42.7 33.4 %all-to-all-start.1 = ((bf16[128,32,128]{2,0,1:T(8,128)(2,1)}), bf16[128,32,128]{2,0,1:T(8,128)(2,1)S(1)}, u32[]{:S(2)}, u32[]{:S(2)}) async-start(bf16[128,32,128]{2,0,1:T(8,128)(2,1)} %bitcast.99), calls=%async_computation.1 | async-start | bytes 2097152 | tf_op jit(solution)/shard_map/all_to_all | solution.py:59
  76.1 33.3 %all-to-all-start = ((bf16[128,32,128]{2,0,1:T(8,128)(2,1)}), bf16[128,32,128]{2,0,1:T(8,128)(2,1)}, u32[]{:S(2)}, u32[]{:S(2)}) async-start(bf16[128,32,128]{2,0,1:T(8,128)(2,1)} %copy_bitcast_fusion.1), calls=%async_computation | async-start | bytes 2097152 | tf_op jit(solution)/shard_map/all_to_all | solution.py:57
  81.1 3.5 copy-start.4
  82.7 32.2 %collective-permute-start = (bf16[2,4096,128]{2,1,0:T(8,128)(2,1)}, bf16[2,4096,128]{2,1,0:T(8,128)(2,1)}, u32[]{:S(2)}, u32[]{:S(2)}) collective-permute-start(bf16[2,4096,128]{2,1,0:T(8,128)(2,1)} %pad_maximum_fusion), channel_id=1, source_target_pairs={{0,32},{32,64},{64,96},{96,128},{128,160},{160,192},{192,224},{224... | collective-permute-start | bytes 6291464 | tf_op jit(solution)/shard_map/ppermute | solution.py:15
  109.4 33.3 %all-to-all-start.3 = ((bf16[128,32,128]{2,0,1:T(8,128)(2,1)}), bf16[128,32,128]{2,0,1:T(8,128)(2,1)}, u32[]{:S(2)}, u32[]{:S(2)}) async-start(bf16[128,32,128]{2,0,1:T(8,128)(2,1)} %copy_bitcast_fusion), calls=%async_computation.3 | async-start | bytes 2097152 | tf_op jit(solution)/shard_map/all_to_all | solution.py:58
  265.5 25.8 %collective-permute-start.1 = (bf16[2,4096,128]{2,1,0:T(8,128)(2,1)}, bf16[2,4096,128]{2,1,0:T(8,128)(2,1)}, u32[]{:S(2)}, u32[]{:S(2)}) collective-permute-start(bf16[2,4096,128]{2,1,0:T(8,128)(2,1)} %pad_maximum_fusion.3), channel_id=1, source_target_pairs={{32,0},{64,32},{96,64},{128,96},{160,128},{192,160},{224,192},{256... | collective-permute-start | bytes 6291464 | tf_op jit(solution)/shard_map/ppermute | solution.py:15
  267.4 32.8 %all-to-all-start.4 = ((bf16[32,128,128]{2,1,0:T(8,128)(2,1)}), bf16[32,128,128]{2,1,0:T(8,128)(2,1)S(1)}, u32[]{:S(2)}, u32[]{:S(2)}) async-start(bf16[32,128,128]{2,1,0:T(8,128)(2,1)} %bitcast.18), calls=%async_computation.4 | async-start | bytes 2097152 | tf_op jit(solution)/shard_map/all_to_all | solution.py:116
  272.3 20.8 %copy-start.1 = (f32[8192,128]{1,0:T(8,128)S(1)}, f32[8192,128]{1,0:T(8,128)}, u32[]{:S(2)}) copy-start(f32[8192,128]{1,0:T(8,128)} %get-tuple-element.261) | copy-start | bytes 12582916
  336.0 33.4 %all-to-all-start.6 = ((bf16[32,128,128]{2,1,0:T(8,128)(2,1)}), bf16[32,128,128]{2,1,0:T(8,128)(2,1)S(1)}, u32[]{:S(2)}, u32[]{:S(2)}) async-start(bf16[32,128,128]{2,1,0:T(8,128)(2,1)} %bitcast.29), calls=%async_computation.6 | async-start | bytes 2097152 | tf_op jit(solution)/shard_map/all_to_all | solution.py:121
  342.5 2.4 copy-start.2
where the time goes:
time: 373 us; the launch traced here: 370 us
  waiting for transfers between devices  147 us (39%)
  matrix products  90.5 us (24%)
  starting transfers between devices  38.9 us (10%)
  blocking collectives  35.8 us (10%)
  local copies, waits for them, and re-layouts  29 us (8%)
  other arithmetic  23.1 us (6%)
  loops' own time  5.39 us (1%)
    all_to_all x1, blocking collectives, local(): lax.all_to_all(as_sent(term_k), 'seq', split_axis=0, concat_axis=1, tiled...  35.8 us
    all_to_all x1, waiting for transfers between devices, local(): lax.all_to_all(spread_v, 'seq', split_axis=1, concat_axis=0, tiled=True)  28.6 us
    all_to_all x1, waiting for transfers between devices, local(): lax.all_to_all(spread_k, 'seq', split_axis=1, concat_axis=0, tiled=True)  27 us
    all_to_all x1, waiting for transfers between devices, local(): lax.all_to_all(d_out, 'seq', split_axis=1, concat_axis=0, tiled=True)  23.9 us
    all_to_all x1, waiting for transfers between devices, local(): lax.all_to_all(as_sent(term_v), 'seq', split_axis=0, concat_axis=1, tiled...  23.5 us
    dot_general x8, matrix products, block_grads(): grad_v = jnp.dot(probs_low.T, grad_rows, preferred_element_type=jnp.float32)  22.3 us
    all_to_all x1, waiting for transfers between devices, local(): lax.all_to_all(queries, 'seq', split_axis=1, concat_axis=0, tiled=True)  21 us
    dot_general x8, matrix products, block_grads(): grad_k = jnp.dot(grad_scores.T, q_rows, preferred_element_type=jnp.float32)  20.4 us
  transfers between devices with their start and end apart: 8, of which 7 were waited for; matrix products, arithmetic and copies ran while one was open for 6% of the time, Pallas kernels for 0%

commit v1 on v0

--- a/solution.py
+++ b/solution.py
@@ -1,3 +1,4 @@
+import functools
 import math
 import jax
 import jax.numpy as jnp
@@ -7,6 +8,22 @@
 HEAD_SIZE = 128
 GROUP = 8
 DOC_MOST = 768
+
+
+def drive_cubes(inputs, dev_axis):
+    plain = jnp.concatenate(
+        lax.all_to_all(
+            jnp.stack(jnp.split(inputs, lax.axis_size(dev_axis), axis=1)),
+            axis_name=dev_axis,
+            split_axis=0,
+            concat_axis=0,
+        ),
+        0,
+    )
+    return plain
+
+
+cut_the_pairs_all = functools.partial(drive_cubes, dev_axis="seq")
 
 
 def from_behind(value, axis, steps):
@@ -57,7 +74,7 @@
         lax.all_to_all(queries, "seq", split_axis=1, concat_axis=0, tiled=True),
         lax.all_to_all(d_out, "seq", split_axis=1, concat_axis=0, tiled=True),
         lax.all_to_all(spread_k, "seq", split_axis=1, concat_axis=0, tiled=True),
-        lax.all_to_all(spread_v, "seq", split_axis=1, concat_axis=0, tiled=True),
+        cut_the_pairs_all(spread_v),
     )
     tail_pair = jnp.stack([head_k, head_v])
     prior_pair = from_behind(tail_pair, "dp", 1)

time: 373 us -> 371 us (level)
    all_to_all x1, starting transfers between devices: 5.07 us -> 9.95 us  [local(): lax.all_to_all(spread_k, 'seq', split_axis=1, concat_axis=0, tiled=True)]
    all_to_all x1, starting transfers between devices: 9.95 us -> 5.07 us  [drive_cubes(): lax.all_to_all(jnp.stack(jnp.split(inputs, lax.axis_size(dev_axis), axis=...]
where the time goes in v1:
time: 371 us; the launch traced here: 369 us
  waiting for transfers between devices  144 us (39%)
  matrix products  90.5 us (24%)
  starting transfers between devices  39 us (11%)
  blocking collectives  35.8 us (10%)
  local copies, waits for them, and re-layouts  30 us (8%)
  other arithmetic  23.1 us (6%)
  loops' own time  5.39 us (1%)
    all_to_all x1, blocking collectives, local(): lax.all_to_all(as_sent(term_k), 'seq', split_axis=0, concat_axis=1, tiled...  35.8 us
    all_to_all x1, waiting for transfers between devices, drive_cubes(): lax.all_to_all(jnp.stack(jnp.split(inputs, lax.axis_size(dev_axis), axis=...  27 us
    all_to_all x1, waiting for transfers between devices, local(): lax.all_to_all(spread_k, 'seq', split_axis=1, concat_axis=0, tiled=True)  26.2 us
    all_to_all x1, waiting for transfers between devices, local(): lax.all_to_all(d_out, 'seq', split_axis=1, concat_axis=0, tiled=True)  23.9 us
    all_to_all x1, waiting for transfers between devices, local(): lax.all_to_all(as_sent(term_v), 'seq', split_axis=0, concat_axis=1, tiled...  23.5 us
    dot_general x8, matrix products, block_grads(): grad_v = jnp.dot(probs_low.T, grad_rows, preferred_element_type=jnp.float32)  22.3 us
    all_to_all x1, waiting for transfers between devices, local(): lax.all_to_all(queries, 'seq', split_axis=1, concat_axis=0, tiled=True)  21 us
    dot_general x8, matrix products, block_grads(): grad_k = jnp.dot(grad_scores.T, q_rows, preferred_element_type=jnp.float32)  20.4 us
  transfers between devices with their start and end apart: 8, of which 7 were waited for; matrix products, arithmetic and copies ran while one was open for 6% of the time, Pallas kernels for 0%

profile of v1, /device:TPU:448, one launch (start us, length us, event | category | flops | bytes accessed | tf_op | source)
XLA Modules:
  0.0 369.2 jit_solution(441683634494273779)
XLA Ops:
  2.9 10.0 %all-to-all-start.1 = ((bf16[128,32,128]{2,0,1:T(8,128)(2,1)}), bf16[128,32,128]{2,0,1:T(8,128)(2,1)S(1)}, u32[]{:S(2)}, u32[]{:S(2)}) async-start(bf16[128,32,128]{2,0,1:T(8,128)(2,1)} %bitcast.6), calls=%async_computation.1 | async-start | bytes 2097152 | tf_op jit(solution)/shard_map/all_to_all | solution.py:76
  15.3 26.2 %all-to-all-done.1 = bf16[128,32,128]{2,0,1:T(8,128)(2,1)S(1)} async-done(((bf16[128,32,128]{2,0,1:T(8,128)(2,1)}), bf16[128,32,128]{2,0,1:T(8,128)(2,1)S(1)}, u32[]{:S(2)}, u32[]{:S(2)}) %all-to-all-start.1) | async-done | bytes 1048608 | tf_op jit(solution)/shard_map/all_to_all | solution.py:76
  41.5 5.1 %all-to-all-start.2 = ((bf16[32,128,128]{2,1,0:T(8,128)(2,1)}), bf16[32,128,128]{2,1,0:T(8,128)(2,1)S(1)}, u32[]{:S(2)}, u32[]{:S(2)}) async-start(bf16[32,128,128]{2,1,0:T(8,128)(2,1)} %copy-done.3), calls=%async_computation.2 | async-start | bytes 2097152 | tf_op jit(solution)/shard_map/all_to_all | solution.py:15
  47.9 27.0 %all-to-all-done.2 = bf16[32,128,128]{2,1,0:T(8,128)(2,1)S(1)} async-done(((bf16[32,128,128]{2,1,0:T(8,128)(2,1)}), bf16[32,128,128]{2,1,0:T(8,128)(2,1)S(1)}, u32[]{:S(2)}, u32[]{:S(2)}) %all-to-all-start.2) | async-done | bytes 1048608 | tf_op jit(solution)/shard_map/all_to_all | solution.py:15
  74.9 5.0 %all-to-all-start = ((bf16[128,32,128]{2,0,1:T(8,128)(2,1)}), bf16[128,32,128]{2,0,1:T(8,128)(2,1)}, u32[]{:S(2)}, u32[]{:S(2)}) async-start(bf16[128,32,128]{2,0,1:T(8,128)(2,1)} %copy_bitcast_fusion.2), calls=%async_computation | async-start | bytes 2097152 | tf_op jit(solution)/shard_map/all_to_all | solution.py:74
  84.7 2.5 copy_bitcast_fusion.1
  87.2 21.0 %all-to-all-done = bf16[128,32,128]{2,0,1:T(8,128)(2,1)} async-done(((bf16[128,32,128]{2,0,1:T(8,128)(2,1)}), bf16[128,32,128]{2,0,1:T(8,128)(2,1)}, u32[]{:S(2)}, u32[]{:S(2)}) %all-to-all-start) | async-done | bytes 1048608 | tf_op jit(solution)/shard_map/all_to_all | solution.py:74
  108.2 5.0 %all-to-all-start.3 = ((bf16[128,32,128]{2,0,1:T(8,128)(2,1)}), bf16[128,32,128]{2,0,1:T(8,128)(2,1)}, u32[]{:S(2)}, u32[]{:S(2)}) async-start(bf16[128,32,128]{2,0,1:T(8,128)(2,1)} %copy_bitcast_fusion.1), calls=%async_computation.3 | async-start | bytes 2097152 | tf_op jit(solution)/shard_map/all_to_all | solution.py:75
  115.3 2.2 pad_maximum_fusion.1
  117.6 23.9 %all-to-all-done.3 = bf16[128,32,128]{2,0,1:T(8,128)(2,1)} async-done(((bf16[128,32,128]{2,0,1:T(8,128)(2,1)}), bf16[128,32,128]{2,0,1:T(8,128)(2,1)}, u32[]{:S(2)}, u32[]{:S(2)}) %all-to-all-start.3) | async-done | bytes 1048608 | tf_op jit(solution)/shard_map/all_to_all | solution.py:75
  141.5 2.2 broadcast_in_dim.52.clone
  143.8 2.2 broadcast_in_dim.52
  146.0 113.3 %while.18 = (s32[]{:T(128)}, f32[8192,128]{1,0:T(8,128)}, f32[8192,128]{1,0:T(8,128)}, bf16[8,512,128]{2,1,0:T(8,128)(2,1)}, s32[8]{0:T(128)S(1)}, /*index=5*/s3...) while((s32[]{:T(128)}, f32[8192,128]{1,0:T(8,128)}, ...), condition=%wide.region_8.9_spmd, body=%wide.region_4.0_spmd.sunk | while | flops 853671680 | bytes 26610516 | solution.py:121
  147.5 2.0 fusion.51
  152.7 2.1 fusion.55
  154.8 2.8 fusion.54
  157.6 2.6 fusion.53
  161.7 2.0 fusion.51
  166.8 2.1 fusion.55
  169.0 2.8 fusion.54
  171.8 2.5 fusion.53
  181.0 2.1 fusion.55
  183.1 2.8 fusion.54
  185.9 2.6 fusion.53
  195.2 2.1 fusion.55
  197.3 2.8 fusion.54
  200.1 2.6 fusion.53
  209.3 2.1 fusion.55
  211.5 2.8 fusion.54
  214.3 2.6 fusion.53
  223.5 2.1 fusion.55
  225.7 2.8 fusion.54
  228.4 2.5 fusion.53
  232.5 2.0 fusion.51
  237.7 2.1 fusion.55
  239.8 2.8 fusion.54
  242.6 2.5 fusion.53
  251.8 2.1 fusion.55
  253.9 2.8 fusion.54
  256.7 2.6 fusion.53
  266.2 4.9 %all-to-all-start.4 = ((bf16[32,128,128]{2,1,0:T(8,128)(2,1)}), bf16[32,128,128]{2,1,0:T(8,128)(2,1)S(1)}, u32[]{:S(2)}, u32[]{:S(2)}) async-start(bf16[32,128,128]{2,1,0:T(8,128)(2,1)} %bitcast.48), calls=%async_computation.4 | async-start | bytes 2097152 | tf_op jit(solution)/shard_map/all_to_all | solution.py:133
  271.1 18.9 %collective-permute-done.1 = bf16[2,4096,128]{2,1,0:T(8,128)(2,1)} collective-permute-done((bf16[2,4096,128]{2,1,0:T(8,128)(2,1)}, bf16[2,4096,128]{2,1,0:T(8,128)(2,1)}, u32[]{:S(2)}, u32[]{:S(2)}) %collective-permute-start.1) | collective-permute-done | bytes 2097184 | tf_op jit(solution)/shard_map/ppermute | solution.py:32
  291.9 3.2 fusion.23
  295.1 3.9 %all-to-all-done.4 = bf16[32,128,128]{2,1,0:T(8,128)(2,1)S(1)} async-done(((bf16[32,128,128]{2,1,0:T(8,128)(2,1)}), bf16[32,128,128]{2,1,0:T(8,128)(2,1)S(1)}, u32[]{:S(2)}, u32[]{:S(2)}) %all-to-all-start.4) | async-done | bytes 1048608 | tf_op jit(solution)/shard_map/all_to_all | solution.py:133
  299.0 35.8 %all_to_all.107 = bf16[32,128,128]{2,1,0:T(8,128)(2,1)} all-to-all(bf16[32,128,128]{2,1,0:T(8,128)(2,1)S(1)} %bitcast.254), channel_id=1, replica_groups=mesh['dp'=16,'seq'=32] {'seq'}, dimensions={0} | all-to-all | bytes 2097152 | tf_op jit(solution)/shard_map/all_to_all | solution.py:135
  334.8 5.1 %all-to-all-start.6 = ((bf16[32,128,128]{2,1,0:T(8,128)(2,1)}), bf16[32,128,128]{2,1,0:T(8,128)(2,1)S(1)}, u32[]{:S(2)}, u32[]{:S(2)}) async-start(bf16[32,128,128]{2,1,0:T(8,128)(2,1)} %bitcast.59), calls=%async_computation.6 | async-start | bytes 2097152 | tf_op jit(solution)/shard_map/all_to_all | solution.py:138
  341.3 2.4 copy.34
  344.7 23.5 %all-to-all-done.6 = bf16[32,128,128]{2,1,0:T(8,128)(2,1)S(1)} async-done(((bf16[32,128,128]{2,1,0:T(8,128)(2,1)}), bf16[32,128,128]{2,1,0:T(8,128)(2,1)S(1)}, u32[]{:S(2)}, u32[]{:S(2)}) %all-to-all-start.6) | async-done | bytes 1048608 | tf_op jit(solution)/shard_map/all_to_all | solution.py:138
  (147 shorter events, 66.7 us)
Async XLA Ops:
  0.6 46.0 %copy-start = (bf16[128,4096]{1,0:T(8,128)(2,1)S(1)}, bf16[128,4096]{1,0:T(8,128)(2,1)}, u32[]{:S(2)}) copy-start(bf16[128,4096]{1,0:T(8,128)(2,1)} %param.7) | copy-start | bytes 3145732
  0.6 12.2 %copy-start.4 = (bf16[128,512]{1,0:T(8,128)(2,1)S(1)}, bf16[128,512]{1,0:T(8,128)(2,1)}, u32[]{:S(2)}) copy-start(bf16[128,512]{1,0:T(8,128)(2,1)} %param.9) | copy-start | bytes 393220
  2.9 38.6 %all-to-all-start.1 = ((bf16[128,32,128]{2,0,1:T(8,128)(2,1)}), bf16[128,32,128]{2,0,1:T(8,128)(2,1)S(1)}, u32[]{:S(2)}, u32[]{:S(2)}) async-start(bf16[128,32,128]{2,0,1:T(8,128)(2,1)} %bitcast.6), calls=%async_computation.1 | async-start | bytes 2097152 | tf_op jit(solution)/shard_map/all_to_all | solution.py:76
  14.3 1.0 copy-start.3
  41.5 33.4 %all-to-all-start.2 = ((bf16[32,128,128]{2,1,0:T(8,128)(2,1)}), bf16[32,128,128]{2,1,0:T(8,128)(2,1)S(1)}, u32[]{:S(2)}, u32[]{:S(2)}) async-start(bf16[32,128,128]{2,1,0:T(8,128)(2,1)} %copy-done.3), calls=%async_computation.2 | async-start | bytes 2097152 | tf_op jit(solution)/shard_map/all_to_all | solution.py:15
  74.9 33.3 %all-to-all-start = ((bf16[128,32,128]{2,0,1:T(8,128)(2,1)}), bf16[128,32,128]{2,0,1:T(8,128)(2,1)}, u32[]{:S(2)}, u32[]{:S(2)}) async-start(bf16[128,32,128]{2,0,1:T(8,128)(2,1)} %copy_bitcast_fusion.2), calls=%async_computation | async-start | bytes 2097152 | tf_op jit(solution)/shard_map/all_to_all | solution.py:74
  79.9 3.5 copy-start.5
  81.5 32.2 %collective-permute-start = (bf16[2,4096,128]{2,1,0:T(8,128)(2,1)}, bf16[2,4096,128]{2,1,0:T(8,128)(2,1)}, u32[]{:S(2)}, u32[]{:S(2)}) collective-permute-start(bf16[2,4096,128]{2,1,0:T(8,128)(2,1)} %pad_maximum_fusion), channel_id=1, source_target_pairs={{0,32},{32,64},{64,96},{96,128},{128,160},{160,192},{192,224},{224... | collective-permute-start | bytes 6291464 | tf_op jit(solution)/shard_map/ppermute | solution.py:32
  108.2 33.3 %all-to-all-start.3 = ((bf16[128,32,128]{2,0,1:T(8,128)(2,1)}), bf16[128,32,128]{2,0,1:T(8,128)(2,1)}, u32[]{:S(2)}, u32[]{:S(2)}) async-start(bf16[128,32,128]{2,0,1:T(8,128)(2,1)} %copy_bitcast_fusion.1), calls=%async_computation.3 | async-start | bytes 2097152 | tf_op jit(solution)/shard_map/all_to_all | solution.py:75
  264.3 25.8 %collective-permute-start.1 = (bf16[2,4096,128]{2,1,0:T(8,128)(2,1)}, bf16[2,4096,128]{2,1,0:T(8,128)(2,1)}, u32[]{:S(2)}, u32[]{:S(2)}) collective-permute-start(bf16[2,4096,128]{2,1,0:T(8,128)(2,1)} %pad_maximum_fusion.3), channel_id=1, source_target_pairs={{32,0},{64,32},{96,64},{128,96},{160,128},{192,160},{224,192},{256... | collective-permute-start | bytes 6291464 | tf_op jit(solution)/shard_map/ppermute | solution.py:32
  266.2 32.8 %all-to-all-start.4 = ((bf16[32,128,128]{2,1,0:T(8,128)(2,1)}), bf16[32,128,128]{2,1,0:T(8,128)(2,1)S(1)}, u32[]{:S(2)}, u32[]{:S(2)}) async-start(bf16[32,128,128]{2,1,0:T(8,128)(2,1)} %bitcast.48), calls=%async_computation.4 | async-start | bytes 2097152 | tf_op jit(solution)/shard_map/all_to_all | solution.py:133
  271.1 20.8 %copy-start.1 = (f32[8192,128]{1,0:T(8,128)S(1)}, f32[8192,128]{1,0:T(8,128)}, u32[]{:S(2)}) copy-start(f32[8192,128]{1,0:T(8,128)} %get-tuple-element.261) | copy-start | bytes 12582916
  334.8 33.4 %all-to-all-start.6 = ((bf16[32,128,128]{2,1,0:T(8,128)(2,1)}), bf16[32,128,128]{2,1,0:T(8,128)(2,1)S(1)}, u32[]{:S(2)}, u32[]{:S(2)}) async-start(bf16[32,128,128]{2,1,0:T(8,128)(2,1)} %bitcast.59), calls=%async_computation.6 | async-start | bytes 2097152 | tf_op jit(solution)/shard_map/all_to_all | solution.py:138
  341.3 2.4 copy-start.2
